TPU v7x, 32 devices: a whole 2x2x4 slice. The times are simulated.
32 devices in a mesh: fsdp: 8 (over z, y), owner: 4 (over x, core).
Axes of the slice: x: 2, y: 2, z: 4, core: 2. Of those that a mesh axis runs over, the one named last changes fastest.
Arguments:
- grads: bfloat16 [32, 1024, 1024], P(None, ('fsdp', 'owner'))
- second_moment: float32 [32, 1024, 1024], P(None, ('fsdp', 'owner')), may hold values from 0.00024414062 to 0.00390625
- assign: int32 [32], replicated, may hold values from 0 to 31, each once
- left_stats: float32 [32, 1024, 1024], P(('fsdp', 'owner')), as said below
- right_stats: float32 [32, 1024, 1024], P(('fsdp', 'owner')), as said below
Outputs:
- update: bfloat16 [32, 1024, 1024], P(None, ('fsdp', 'owner'))
- left_new: float32 [32, 1024, 1024], P(('fsdp', 'owner'))
- right_new: float32 [32, 1024, 1024], P(('fsdp', 'owner'))
Inputs may be any that keep to these rules, and one draw needn't show every extreme that they name: assign is a permutation of the 32 blocks; slot s holds block assign[s], and each device owns a run of 1 slots. `left_stats`: each block is symmetric positive definite. `right_stats`: each block is symmetric positive definite.
All inputs are finite; a program needn't handle non-finite values.
Results may differ from a plain program's by a relative error of at most 0.001.
The roundings to bfloat16 on the way count: a program that leaves them out, or rounds other values in their place, can miss the bound.
Values may be sent and summed in bfloat16 or wider, within the bound.
A program may use at most 128 MiB of HBM per device.

v0:
```python
import jax
import jax.numpy as jnp
from jax import lax
from jax.sharding import PartitionSpec as P

ITERS = 2


def inverse_root(factor):
    dimension = factor.shape[0]
    identity = jnp.eye(dimension, dtype=jnp.float32)
    frob_norm = jnp.sqrt(jnp.sum(factor * factor))
    ns_matrix = factor / frob_norm
    root_now = identity
    for sweep in range(ITERS):
        newton_mix = (5.0 * identity - ns_matrix) * 0.25
        mix_low = newton_mix.astype(jnp.bfloat16)
        if sweep == 0:
            root_now = frob_norm ** (-0.25) * newton_mix
        else:
            root_now = jnp.dot(
                root_now.astype(jnp.bfloat16), mix_low, preferred_element_type=jnp.float32
            )
        if sweep < ITERS - 1:
            square = jnp.dot(mix_low, mix_low, preferred_element_type=jnp.float32).astype(
                jnp.bfloat16
            )
            fourth = jnp.dot(square, square, preferred_element_type=jnp.float32).astype(
                jnp.bfloat16
            )
            ns_matrix = jnp.dot(
                fourth, ns_matrix.astype(jnp.bfloat16), preferred_element_type=jnp.float32
            )
    return root_now.astype(jnp.bfloat16)


def owner_update(grad_block, left_stat, right_stat, adam_sq):
    identity = jnp.eye(grad_block.shape[0], dtype=jnp.float32)
    left_full = (
        0.9 * left_stat
        + 0.1 * jnp.dot(grad_block, grad_block.T, preferred_element_type=jnp.float32)
        + 0.0001 * identity
    )
    right_full = (
        0.9 * right_stat
        + 0.1 * jnp.dot(grad_block.T, grad_block, preferred_element_type=jnp.float32)
        + 0.0001 * identity
    )
    left_root = inverse_root(left_full)
    right_root = inverse_root(right_full)
    left_applied = jnp.dot(left_root, grad_block, preferred_element_type=jnp.float32).astype(
        jnp.bfloat16
    )
    precond = jnp.dot(left_applied, right_root, preferred_element_type=jnp.float32)
    precond_sq = jnp.mean(precond * precond)
    precond_low = lax.optimization_barrier(precond.astype(jnp.bfloat16))
    scaled = precond_low.astype(jnp.float32) * (jnp.sqrt(adam_sq) / jnp.sqrt(precond_sq + 1e-06))
    return (scaled.astype(jnp.bfloat16), left_full, right_full)


def adam_squares(grad_part, moment_part):
    grad_wide = grad_part.astype(jnp.float32)
    moment = 0.9 * moment_part + 0.1 * grad_wide * grad_wide
    adam_dir = grad_wide / (jnp.sqrt(moment) + 1e-08)
    return jnp.sum(adam_dir * adam_dir, axis=(1, 2))


def local(grads, second_moment, assign, left_stats, right_stats):
    row_count = grads.shape[1]
    block_width = grads.shape[2]
    owned_count = left_stats.shape[0]
    fsdp_count = lax.axis_size("fsdp")
    owner_count = lax.axis_size("owner")
    rank_count = fsdp_count * owner_count
    outgoing = grads[assign]
    received = lax.all_to_all(outgoing, ("fsdp", "owner"), split_axis=0, concat_axis=1, tiled=True)
    moments_in = lax.all_to_all(
        second_moment[assign].astype(jnp.bfloat16),
        ("fsdp", "owner"),
        split_axis=0,
        concat_axis=1,
        tiled=True,
    ).astype(jnp.float32)
    adam_sq = adam_squares(received, moments_in) / (block_width * block_width)

    def slot_work(slot_item):
        return owner_update(slot_item[0], slot_item[1], slot_item[2], slot_item[3])

    slot_updates, left_new, right_new = lax.map(
        slot_work, (received, left_stats, right_stats, adam_sq)
    )
    returning = slot_updates.reshape(owned_count, rank_count, row_count, block_width)
    arrived = lax.all_to_all(returning, ("fsdp", "owner"), split_axis=1, concat_axis=0, tiled=True)
    arrived = arrived.reshape(rank_count * owned_count, row_count, block_width)
    update = jnp.zeros_like(grads).at[assign].set(arrived)
    return (update, left_new, right_new)


def solution(mesh):
    placed = (
        P(None, ("fsdp", "owner"), None),
        P(None, ("fsdp", "owner"), None),
        P(),
        P(("fsdp", "owner"), None, None),
        P(("fsdp", "owner"), None, None),
    )
    return jax.shard_map(
        local,
        mesh=mesh,
        in_specs=placed,
        out_specs=(
            P(None, ("fsdp", "owner"), None),
            P(("fsdp", "owner"), None, None),
            P(("fsdp", "owner"), None, None),
        ),
        check_vma=False,
    )
```

profile of v0, /device:TPU:0, one launch (start us, length us, event | category | flops | bytes accessed | tf_op | source)
XLA Modules:
  0.0 258.5 jit_solution(10110047014219482263)
XLA Ops:
  0.6 0.0 copy-start
  0.6 0.8 compare_select_fusion
  1.5 4.3 %gather_fusion.1 = bf16[32,32,1024]{2,1,0:T(8,128)(2,1)} fusion(f32[32,32,1024]{2,1,0:T(8,128)} %param.6, s32[1024]{0:T(1024)S(1)} %pad_clamp_fusion), kind=kCustom, calls=%fused_computation.1 | custom fusion | bytes 4194432 | tf_op jit(solution)/shard_map/gather | solution.py:78
  5.7 7.4 %all-to-all-start.1 = ((bf16[32,32,1024]{2,1,0:T(8,128)(2,1)}), bf16[32,32,1024]{2,1,0:T(8,128)(2,1)}, u32[]{:S(2)}, u32[]{:S(2)}) async-start(bf16[32,32,1024]{2,1,0:T(8,128)(2,1)} %gather_fusion.1), calls=%async_computation.1 | async-start | bytes 4194304 | tf_op jit(solution)/shard_map/all_to_all | solution.py:77
  13.1 0.0 copy-done
  13.2 2.0 gather_fusion
  15.2 46.9 %all-to-all-done.1 = bf16[32,32,1024]{2,1,0:T(8,128)(2,1)} async-done(((bf16[32,32,1024]{2,1,0:T(8,128)(2,1)}), bf16[32,32,1024]{2,1,0:T(8,128)(2,1)}, u32[]{:S(2)}, u32[]{:S(2)}) %all-to-all-start.1) | async-done | bytes 2097184 | tf_op jit(solution)/shard_map/all_to_all | solution.py:77
  62.0 52.7 %all_to_all.12 = bf16[32,32,1024]{2,1,0:T(8,128)(2,1)S(1)} all-to-all(bf16[32,32,1024]{2,1,0:T(8,128)(2,1)} %gather_fusion), channel_id=1, replica_groups=mesh['fsdp'=8,'owner'=4] {'fsdp','owner'}, dimensions={0} | all-to-all | bytes 4194304 | tf_op jit(solution)/shard_map/all_to_all | solution.py:76
  114.7 0.0 copy-start.1
  114.7 1.3 copy-done.1
  116.1 4.6 %fusion.9 = f32[]{:T(128)} fusion(bf16[32,32,1024]{2,1,0:T(8,128)(2,1)} %all-to-all-done.1, bf16[32,32,1024]{2,1,0:T(8,128)(2,1)S(1)} %all_to_all.12), kind=kLoop, calls=%fused_computation.31 | loop fusion | flops 10485759 | bytes 4194308 | tf_op jit(solution)/shard_map/reduce_sum | solution.py:65
  121.4 8.6 %multiply_reduce_fusion.2 = (f32[]{:T(128)}, f32[1024,1024]{1,0:T(8,128)}) fusion(bf16[1024,1024]{1,0:T(8,128)(2,1)} %bitcast.31, f32[1,1024,1024]{2,1,0:T(8,128)} %param.8), kind=kOutput, calls=%fused_computation.29 | convolution fusion | flops 2155872256 | bytes 10485764 | tf_op jit(solution)/shard_map/while/body/eval_jaxpr/dot_general | solution.py:41
  130.8 7.2 %fusion.11 = bf16[1024,1024]{1,0:T(8,128)(2,1)} fusion(f32[1024,1024]{1,0:T(8,128)} %get-tuple-element.22, f32[]{:T(128)S(6)} %sqrt.24), kind=kOutput, calls=%fused_computation.33 | convolution fusion | flops 2153775104 | bytes 6291460 | tf_op jit(solution)/shard_map/while/body/eval_jaxpr/dot_general | solution.py:25
  137.9 9.9 %fusion.27 = f32[1024,1024]{1,0:T(8,128)} fusion(bf16[1024,1024]{1,0:T(8,128)(2,1)} %fusion.11, f32[1024,1024]{1,0:T(8,128)} %get-tuple-element.22, f32[]{:T(128)S(6)} %sqrt.24), kind=kOutput, calls=%fused_computation.48 | convolution fusion | flops 4298113024 | bytes 10485764 | tf_op jit(solution)/shard_map/while/body/eval_jaxpr/dot_general | solution.py:31
  147.8 9.1 %multiply_reduce_fusion.1 = (f32[]{:T(128)}, f32[1024,1024]{1,0:T(8,128)}) fusion(bf16[32,32,1024]{2,1,0:T(8,128)(2,1)} %copy-done.1, f32[1,1024,1024]{2,1,0:T(8,128)} %param.9), kind=kOutput, calls=%fused_computation.26 | convolution fusion | flops 2155872256 | bytes 10485764 | tf_op jit(solution)/shard_map/while/body/eval_jaxpr/dot_general | solution.py:46
  157.6 7.2 %fusion.13 = bf16[1024,1024]{1,0:T(8,128)(2,1)} fusion(f32[1024,1024]{1,0:T(8,128)} %get-tuple-element.32, f32[]{:T(128)S(6)} %sqrt.25), kind=kOutput, calls=%fused_computation.35 | convolution fusion | flops 2153775104 | bytes 6291460 | tf_op jit(solution)/shard_map/while/body/eval_jaxpr/dot_general | solution.py:25
  164.9 9.9 %fusion.18 = f32[1024,1024]{1,0:T(8,128)} fusion(bf16[1024,1024]{1,0:T(8,128)(2,1)} %fusion.13, f32[1024,1024]{1,0:T(8,128)} %get-tuple-element.32, f32[]{:T(128)S(6)} %sqrt.25), kind=kOutput, calls=%fused_computation.38 | convolution fusion | flops 4298113024 | bytes 10485764 | tf_op jit(solution)/shard_map/while/body/eval_jaxpr/dot_general | solution.py:31
  174.8 10.0 %fusion.25 = bf16[1024,1024]{1,0:T(8,128)(2,1)} fusion(bf16[1024,1024]{1,0:T(8,128)(2,1)} %bitcast.32, f32[1024,1024]{1,0:T(8,128)} %fusion.27, f32[]{:T(128)S(6)} %mul.134, f32[1024,1024]{1,0:T(8,128)} %get-tuple-element.22, f32[]{:T(128)S(6)} %sqrt.24), kind=kOutput, calls=%fused_computation.46 | convolution fusion | flops 4307550208 | bytes 12582920 | tf_op jit(solution)/shard_map/while/body/eval_jaxpr/dot_general | solution.py:51
  184.8 10.8 %multiply_reduce_fusion = (f32[]{:T(128)}, bf16[1024,1024]{1,0:T(8,128)(2,1)}) fusion(bf16[1024,1024]{1,0:T(8,128)(2,1)} %fusion.25, f32[1024,1024]{1,0:T(8,128)} %fusion.18, f32[]{:T(128)S(6)} %mul.143, f32[1024,1024]{1,0:T(8,128)} %get-tuple-element.32, f32[]{:T(128)S(6)} %sqrt.25), kind=kOutput, calls=%fused_computation.23 | convolution fusion | flops 4310695936 | bytes 12582924 | tf_op jit(solution)/shard_map/while/body/eval_jaxpr/dot_general | solution.py:54
  196.4 2.1 multiply_convert_fusion
  198.5 52.3 %all_to_all.13 = bf16[1,32,32,1024]{3,2,0,1:T(8,128)(2,1)} all-to-all(bf16[1,32,32,1024]{3,2,0,1:T(8,128)(2,1)S(1)} %bitcast.33), channel_id=1, replica_groups=mesh['fsdp'=8,'owner'=4] {'fsdp','owner'}, dimensions={1} | all-to-all | bytes 4194304 | tf_op jit(solution)/shard_map/all_to_all | solution.py:93
  250.8 1.6 broadcast_in_dim.21
  252.3 6.2 %scatter_fusion = bf16[32,32,1024]{2,1,0:T(8,128)(2,1)} fusion(bf16[32,32,1024]{2,1,0:T(8,128)(2,1)} %broadcast_in_dim.21, s32[32]{0:T(128)S(1)} %compare_select_fusion, bf16[32,32,1024]{2,1,0:T(8,128)(2,1)} %bitcast.30), kind=kCustom, calls=%fused_computation.2 | custom fusion | bytes 6291584 | tf_op jit(solution)/shard_map/scatter | solution.py:95
  (1 shorter events, 0.0 us)
Async XLA Ops:
  0.6 12.5 %copy-start = (bf16[32,32,1024]{2,1,0:T(8,128)(2,1)S(1)}, bf16[32,32,1024]{2,1,0:T(8,128)(2,1)}, u32[]{:S(2)}) copy-start(bf16[32,32,1024]{2,1,0:T(8,128)(2,1)} %param.5) | copy-start | bytes 6291460
  5.7 56.3 %all-to-all-start.1 = ((bf16[32,32,1024]{2,1,0:T(8,128)(2,1)}), bf16[32,32,1024]{2,1,0:T(8,128)(2,1)}, u32[]{:S(2)}, u32[]{:S(2)}) async-start(bf16[32,32,1024]{2,1,0:T(8,128)(2,1)} %gather_fusion.1), calls=%async_computation.1 | async-start | bytes 4194304 | tf_op jit(solution)/shard_map/all_to_all | solution.py:77
  114.7 1.3 copy-start.1
where the time goes:
time: 259 us
  blocking collectives  105 us (41%)
  matrix products  72.8 us (28%)
  waiting for transfers between devices  46.9 us (18%)
  local copies, waits for them, and re-layouts  15.4 us (6%)
  other arithmetic  7.53 us (3%)
  starting transfers between devices  7.43 us (3%)
  between operations  3.56 us (1%)
    all_to_all x1, blocking collectives, local(): lax.all_to_all(outgoing, ('fsdp', 'owner'), split_axis=0, concat_axis=1,...  52.7 us
    all_to_all x1, blocking collectives, local(): lax.all_to_all(returning, ('fsdp', 'owner'), split_axis=1, concat_axis=0,...  52.3 us
    all_to_all x1, waiting for transfers between devices, local(): lax.all_to_all(second_moment[assign].astype(jnp.bfloat16), ('fsdp', 'owne...  46.9 us
    dot_general x2, matrix products, inverse_root(): jnp.dot(fourth, ns_matrix.astype(jnp.bfloat16), preferred_element_type=jn...  19.8 us
    dot_general x2, matrix products, inverse_root(): jnp.dot(mix_low, mix_low, preferred_element_type=jnp.float32)  14.4 us
    dot_general x1, matrix products, owner_update(): jnp.dot(left_applied, right_root, preferred_element_type=jnp.float32)  10.8 us
    dot_general x1, matrix products, owner_update(): jnp.dot(left_root, grad_block, preferred_element_type=jnp.float32)  9.99 us
    dot_general x1, matrix products, owner_update(): jnp.dot(grad_block.T, grad_block, preferred_element_type=jnp.float32)  9.09 us
  transfers between devices with their start and end apart: 1, of which 1 were waited for; matrix products, arithmetic and copies ran while one was open for 1% of the time, Pallas kernels for 0%

commit v1 on v0

v1 whole, which is shorter than its diff:
```python
import functools

import jax
import jax.numpy as jnp
from jax import lax
from jax.experimental import pallas as pl
from jax.experimental.pallas import tpu as pltpu
from jax.sharding import PartitionSpec as P

MESH = pl.DeviceIdType.MESH
ANY = pl.BlockSpec(memory_space=pl.ANY)
VMEM = pl.BlockSpec(memory_space=pltpu.VMEM)
SMEM = pl.BlockSpec(memory_space=pltpu.SMEM)
F32 = jnp.float32
BF16 = jnp.bfloat16


def dot(a, b):
    return jnp.dot(a, b, preferred_element_type=F32)


def peer_at(fsdp_count, owner_count, step):
    fsdp_off = lax.rem(step // owner_count + fsdp_count // 2, fsdp_count)
    owner_off = lax.rem(step, owner_count)
    fsdp = lax.rem(lax.axis_index("fsdp") + fsdp_off, fsdp_count)
    owner = lax.rem(lax.axis_index("owner") + owner_off, owner_count)
    return fsdp, owner


def exchange(fsdp_count, owner_count, x_ref, o_ref, send_sem, recv_sem, own_sem, between):
    count = fsdp_count * owner_count
    me = lax.axis_index("fsdp") * owner_count + lax.axis_index("owner")
    own_step = (fsdp_count - fsdp_count // 2) * owner_count

    def others(action):
        def body(step, carry):
            action(step)
            return carry

        lax.fori_loop(0, own_step, body, 0)
        lax.fori_loop(own_step + 1, count, body, 0)

    def copy(step):
        fsdp, owner = peer_at(fsdp_count, owner_count, step)
        return pltpu.make_async_remote_copy(
            src_ref=x_ref.at[fsdp * owner_count + owner],
            dst_ref=o_ref.at[me],
            send_sem=send_sem.at[step],
            recv_sem=recv_sem.at[step],
            device_id=(fsdp, owner),
            device_id_type=MESH,
        )

    barrier = pltpu.get_barrier_semaphore()

    def greet(step):
        pl.semaphore_signal(
            barrier, inc=1, device_id=peer_at(fsdp_count, owner_count, step), device_id_type=MESH
        )

    others(greet)
    own = pltpu.make_async_copy(x_ref.at[me], o_ref.at[me], own_sem)
    own.start()
    pl.semaphore_wait(barrier, count - 1)
    others(lambda step: copy(step).start())
    between()
    own.wait()
    others(lambda step: copy(step).wait())


def gather_kernel(
    fsdp_count, owner_count, x_ref, g_hbm, m_hbm, o_ref, sums_ref,
    g_ref, m_ref, send_sem, recv_sem, own_sem, load_sem,
):
    loads = [
        pltpu.make_async_copy(g_hbm, g_ref, load_sem.at[0]),
        pltpu.make_async_copy(m_hbm, m_ref, load_sem.at[1]),
    ]
    for load in loads:
        load.start()

    def adam():
        for load in loads:
            load.wait()

        def body(block, carry):
            wide = g_ref[block].astype(F32)
            moment = 0.9 * m_ref[block] + 0.1 * wide * wide
            adam_dir = wide / (jnp.sqrt(moment) + 1e-08)
            row = jnp.sum(adam_dir * adam_dir, axis=0, keepdims=True)
            sums_ref[pl.ds(block, 1), :] = row
            return carry

        lax.fori_loop(0, g_ref.shape[0], body, 0)

    exchange(fsdp_count, owner_count, x_ref, o_ref, send_sem, recv_sem, own_sem, adam)


def return_kernel(fsdp_count, owner_count, x_ref, o_ref, send_sem, recv_sem, own_sem):
    exchange(
        fsdp_count, owner_count, x_ref, o_ref, send_sem, recv_sem, own_sem, lambda: None
    )


def exchange_scratch(count):
    return [
        pltpu.SemaphoreType.DMA((count,)),
        pltpu.SemaphoreType.DMA((count,)),
        pltpu.SemaphoreType.DMA,
    ]


def gather_rows(outgoing, grads, second_moment, fsdp_count, owner_count):
    count = fsdp_count * owner_count
    return pl.pallas_call(
        functools.partial(gather_kernel, fsdp_count, owner_count),
        out_shape=(
            jax.ShapeDtypeStruct(outgoing.shape, BF16),
            jax.ShapeDtypeStruct((grads.shape[0], grads.shape[2]), F32),
        ),
        in_specs=[ANY, ANY, ANY],
        out_specs=(ANY, VMEM),
        scratch_shapes=[
            pltpu.VMEM(grads.shape, BF16),
            pltpu.VMEM(second_moment.shape, F32),
        ]
        + exchange_scratch(count)
        + [pltpu.SemaphoreType.DMA((2,))],
        compiler_params=pltpu.CompilerParams(
            collective_id=0, has_side_effects=True, vmem_limit_bytes=24 << 20
        ),
        name="gather_rows",
    )(outgoing, grads, second_moment)


def return_rows(blocks, fsdp_count, owner_count):
    return pl.pallas_call(
        functools.partial(return_kernel, fsdp_count, owner_count),
        out_shape=jax.ShapeDtypeStruct(blocks.shape, BF16),
        in_specs=[ANY],
        out_specs=ANY,
        scratch_shapes=exchange_scratch(fsdp_count * owner_count),
        compiler_params=pltpu.CompilerParams(collective_id=1, has_side_effects=True),
        name="return_rows",
    )(blocks)


def owner_kernel(
    g_ref, ls_hbm, rs_hbm, ln_hbm, rn_hbm, out_ref, sq_ref,
    ls, rs, gt, low, mix, square, fourth, root, load_sem, store_sem,
):
    size = g_ref.shape[0]
    tile = size // 2
    tiles = size // tile
    stats = (ls, rs)
    loads = [
        pltpu.make_async_copy(ls_hbm, ls, load_sem.at[0]),
        pltpu.make_async_copy(rs_hbm, rs, load_sem.at[1]),
    ]
    for load in loads:
        load.start()

    def diagonal(step, height):
        rows = lax.broadcasted_iota(jnp.int32, (height, size), 0) + step * height
        cols = lax.broadcasted_iota(jnp.int32, (height, size), 1)
        return rows == cols

    def rows_of(step, height=tile):
        return pl.ds(pl.multiple_of(step * height, height), height)

    gt[...] = g_ref[...].T
    for load in loads:
        load.wait()

    def gram(step, carry):
        here = rows_of(step)
        eye = jnp.where(diagonal(step, tile), 0.0001, 0.0).astype(F32)
        left = 0.9 * ls[here, :] + 0.1 * dot(g_ref[here, :], gt[...]) + eye
        ls[here, :] = left
        right = 0.9 * rs[here, :] + 0.1 * dot(gt[here, :], g_ref[...]) + eye
        rs[here, :] = right
        return (
            carry[0] + jnp.sum(left * left, axis=0, keepdims=True),
            carry[1] + jnp.sum(right * right, axis=0, keepdims=True),
        )

    zero = jnp.zeros((1, size), F32)
    sums = lax.fori_loop(0, tiles, gram, (zero, zero))
    stores = [
        pltpu.make_async_copy(ls, ln_hbm, store_sem.at[0]),
        pltpu.make_async_copy(rs, rn_hbm, store_sem.at[1]),
    ]
    for store in stores:
        store.start()
    frobs = [jnp.sqrt(jnp.sum(total, axis=1, keepdims=True)) for total in sums]
    inverses = [1.0 / frob for frob in frobs]
    scales = [lax.rsqrt(jnp.sqrt(frob)) for frob in frobs]

    def first(step, carry):
        here = rows_of(step, 128)
        eye = jnp.where(diagonal(step, 128), 5.0, 0.0).astype(F32)
        for side in range(2):
            matrix = stats[side][here, :] * inverses[side]
            newton = (eye - matrix) * 0.25
            low[side, here, :] = matrix.astype(BF16)
            mix[side, here, :] = newton.astype(BF16)
            root[side, here, :] = (scales[side] * newton).astype(BF16)
        return carry

    lax.fori_loop(0, size // 128, first, 0)

    def product(a, b, out, finish):
        def body(step, carry):
            here = rows_of(step)
            for side in range(2):
                out[side, here, :] = finish(step, dot(a[side, here, :], b[side])).astype(BF16)
            return carry

        lax.fori_loop(0, tiles, body, 0)

    def as_is(step, value):
        return value

    def newton_mix(step, value):
        return (jnp.where(diagonal(step, tile), 5.0, 0.0).astype(F32) - value) * 0.25

    product(mix, mix, square, as_is)
    product(square, square, fourth, as_is)
    product(fourth, low, mix, newton_mix)
    product(root, mix, square, as_is)

    def apply_left(step, carry):
        here = rows_of(step)
        gt[here, :] = dot(square[0, here, :], g_ref[...]).astype(BF16)
        return carry

    lax.fori_loop(0, tiles, apply_left, 0)

    def apply_right(step, carry):
        here = rows_of(step)
        value = dot(gt[here, :], square[1])
        out_ref[here, :] = value.astype(BF16)
        return carry + jnp.sum(value * value, axis=0, keepdims=True)

    sq_ref[...] = lax.fori_loop(0, tiles, apply_right, zero)
    for store in stores:
        store.wait()


def owner_update(block, left_stat, right_stat):
    shape = block.shape
    pair = (2,) + shape
    return pl.pallas_call(
        owner_kernel,
        out_shape=(
            jax.ShapeDtypeStruct(shape, F32),
            jax.ShapeDtypeStruct(shape, F32),
            jax.ShapeDtypeStruct(shape, BF16),
            jax.ShapeDtypeStruct((1, shape[1]), F32),
        ),
        in_specs=[VMEM, ANY, ANY],
        out_specs=(ANY, ANY, VMEM, VMEM),
        scratch_shapes=[
            pltpu.VMEM(shape, F32),
            pltpu.VMEM(shape, F32),
            pltpu.VMEM(shape, BF16),
            pltpu.VMEM(pair, BF16),
            pltpu.VMEM(pair, BF16),
            pltpu.VMEM(pair, BF16),
            pltpu.VMEM(pair, BF16),
            pltpu.VMEM(pair, BF16),
            pltpu.SemaphoreType.DMA((2,)),
            pltpu.SemaphoreType.DMA((2,)),
        ],
        compiler_params=pltpu.CompilerParams(vmem_limit_bytes=56 << 20),
        name="owner_update",
    )(block, left_stat, right_stat)


def place_kernel(assign_ref, level_ref, x_ref, o_ref):
    count = x_ref.shape[0]

    def body(slot, carry):
        block = assign_ref[slot]
        scale = level_ref[block] * level_ref[count + slot]
        o_ref[block] = (x_ref[slot].astype(F32) * scale).astype(BF16)
        return carry

    lax.fori_loop(0, count, body, 0)


def place_rows(assign, levels, arrived):
    return pl.pallas_call(
        place_kernel,
        out_shape=jax.ShapeDtypeStruct(arrived.shape, BF16),
        in_specs=[SMEM, SMEM, VMEM],
        out_specs=VMEM,
        compiler_params=pltpu.CompilerParams(vmem_limit_bytes=24 << 20),
        name="place_rows",
    )(assign, levels, arrived)


def local(fsdp_count, owner_count, grads, second_moment, assign, left_stats, right_stats):
    count = fsdp_count * owner_count
    size = grads.shape[2]
    me = lax.axis_index("fsdp") * owner_count + lax.axis_index("owner")
    received, sums = gather_rows(grads[assign], grads, second_moment, fsdp_count, owner_count)
    left_new, right_new, precond_low, squares = owner_update(
        received.reshape(size, size), left_stats[0], right_stats[0]
    )
    arrived = return_rows(precond_low.reshape(grads.shape), fsdp_count, owner_count)
    mine = jnp.where(jnp.arange(count) == me, jnp.sum(squares), 0.0)
    totals = lax.psum(jnp.concatenate([jnp.sum(sums, axis=1), mine]), ("fsdp", "owner"))
    means = totals / (size * size)
    levels = jnp.where(
        jnp.arange(2 * count) < count, jnp.sqrt(means), 1.0 / jnp.sqrt(means + 1e-06)
    )
    update = place_rows(assign, levels, arrived)
    return (update, left_new[None], right_new[None])


def solution(mesh):
    rows = P(None, ("fsdp", "owner"), None)
    blocks = P(("fsdp", "owner"), None, None)
    return jax.shard_map(
        functools.partial(local, mesh.shape["fsdp"], mesh.shape["owner"]),
        mesh=mesh,
        in_specs=(rows, rows, P(), blocks, blocks),
        out_specs=(rows, blocks, blocks),
        check_vma=False,
    )
```

time: 259 us -> 200 us (0.77)
  Pallas kernels: 0 us -> 147 us
  matrix products: 72.8 us -> 0 us
  blocking collectives: 105 us -> 39 us
  waiting for transfers between devices: 46.9 us -> 0 us
  starting transfers between devices: 7.43 us -> 0 us
  local copies, waits for them, and re-layouts: 15.4 us -> 10.4 us
  other arithmetic: 7.53 us -> 2.82 us
  between operations: 3.56 us -> 0.71 us
    pallas_call x0 -> x4, Pallas kernels: none -> 147 us  [the longest x1 54.5 us: gather_rows(): pl.pallas_call(functools.partial(gather_kernel, fsdp_count, owner_count),...]
    all_to_all x2 -> x0, blocking collectives: 105 us -> none  [the longest x1 52.7 us: local(): lax.all_to_all(outgoing, ('fsdp', 'owner'), split_axis=0, concat_axis=1,...]
    dot_general x8 -> x0, matrix products: 72.8 us -> none  [the longest x2 19.8 us: inverse_root(): jnp.dot(fourth, ns_matrix.astype(jnp.bfloat16), preferred_element_type=jn...]
    all_to_all x1 -> x0, waiting for transfers between devices: 46.9 us -> none  [local(): lax.all_to_all(second_moment[assign].astype(jnp.bfloat16), ('fsdp', 'owne...]
    psum x0 -> x1, blocking collectives: none -> 39 us  [local(): lax.psum(jnp.concatenate([jnp.sum(sums, axis=1), mine]), ('fsdp', 'owner'))]
    all_to_all x1 -> x0, starting transfers between devices: 7.43 us -> none  [local(): lax.all_to_all(second_moment[assign].astype(jnp.bfloat16), ('fsdp', 'owne...]
    scatter x1 -> x0, local copies, waits for them, and re-layouts: 6.2 us -> none  [local(): update = jnp.zeros_like(grads).at[assign].set(arrived)]
    unnamed x4 -> x12, local copies, waits for them, and re-layouts: 1.33 us -> 6.69 us
  transfers between devices with their start and end apart: 1 -> 0, of which waited for: 1 -> 0; matrix products, arithmetic and copies ran while one was open for 1% -> 0% of each run, Pallas kernels for 0% -> 0%
where the time goes in v1:
time: 200 us
  Pallas kernels  147 us (74%)
  blocking collectives  39 us (20%)
  local copies, waits for them, and re-layouts  10.4 us (5%)
  other arithmetic  2.82 us (1%)
    pallas_call x1, Pallas kernels, gather_rows(): pl.pallas_call(functools.partial(gather_kernel, fsdp_count, owner_count),...  54.5 us
    pallas_call x1, Pallas kernels, return_rows(): pl.pallas_call(functools.partial(return_kernel, fsdp_count, owner_count),...  52.3 us
    psum x1, blocking collectives, local(): lax.psum(jnp.concatenate([jnp.sum(sums, axis=1), mine]), ('fsdp', 'owner'))  39 us
    pallas_call x1, Pallas kernels, owner_update(): pl.pallas_call(owner_kernel, out_shape=(jax.ShapeDtypeStruct(shape, F32),...  38 us
    unnamed x12, local copies, waits for them, and re-layouts  6.69 us

profile of v1, /device:TPU:0, one launch (start us, length us, event | category | flops | bytes accessed | tf_op | source)
XLA Modules:
  0.0 200.1 jit_solution(16653391787931609369)
XLA Ops:
  0.6 0.7 compare_select_fusion
  1.3 0.0 copy-start.1
  1.3 3.7 %gather_fusion = bf16[32,32,1024]{2,1,0:T(8,128)(2,1)} fusion(bf16[32,32,1024]{2,1,0:T(8,128)(2,1)} %g_hbm.1, s32[1024]{0:T(1024)S(1)} %pad_clamp_fusion), kind=kCustom, calls=%fused_computation | custom fusion | bytes 4194432 | tf_op jit(solution)/shard_map/gather | solution.py:307
  5.0 0.0 copy-done.1
  5.1 0.0 copy-start.2
  5.1 1.6 copy-done.2
  6.6 0.0 copy-start.3
  6.6 2.2 %copy-done.3 = f32[32,32,1024]{2,1,0:T(8,128)S(1)} copy-done((f32[32,32,1024]{2,1,0:T(8,128)S(1)}, f32[32,32,1024]{2,1,0:T(8,128)}, u32[]{:S(2)}) %copy-start.3) | copy-done | bytes 4194328
  8.8 54.5 %gather_rows.1 = (bf16[32,32,1024]{2,1,0:T(8,128)(2,1)S(1)}, f32[32,1024]{1,0:T(8,128)S(1)}) custom-call(bf16[32,32,1024]{2,1,0:T(8,128)(2,1)S(1)} %copy-done.2, bf16[32,32,1024]{2,1,0:T(8,128)(2,1)S(1)} %copy-done.1, f32[32,32,1024]{2,1,0:T(8,128)S(1)} %copy-done.3), custom_call_target="tpu_custom_call" | custom-call | tf_op jit(solution)/shard_map/gather_rows/pallas_call | solution.py:115
  63.3 0.0 copy-start.4
  63.3 1.3 copy-done.4
  64.6 0.1 reduce_sum.18
  64.8 38.0 %owner_update.1 = (f32[1024,1024]{1,0:T(8,128)}, f32[1024,1024]{1,0:T(8,128)}, bf16[1024,1024]{1,0:T(8,128)(2,1)}, f32[1,1024]{1,0:T(1,128)}) custom-call(bf16[1024,1024]{1,0:T(8,128)(2,1)} %bitcast.6, f32[1024,1024]{1,0:T(8,128)} %bitcast.7, f32[1024,1024]{1,0:T(8,128)} %bitcast.8), custom_call_target="tpu_custom_call" | custom-call | tf_op jit(solution)/shard_map/owner_update/pallas_call | solution.py:253
  102.8 1.3 reduce_sum.19
  104.1 0.6 compare_select_fusion.1
  104.7 0.1 pad_maximum_fusion
  104.8 39.0 %psum.7 = f32[64]{0:T(128)S(1)} all-reduce(f32[64]{0:T(128)S(1)} %pad_maximum_fusion), channel_id=1, replica_groups=mesh['fsdp'=8,'owner'=4] {'fsdp','owner'}, use_global_device_ids=true, to_apply=%region_2.3 | all-reduce | flops 64 | bytes 512 | tf_op jit(solution)/shard_map/psum | solution.py:313
  143.8 0.0 copy-start.5
  143.8 52.3 %return_rows.1.x_ref = bf16[32,32,1024]{2,1,0:T(8,128)(2,1)} custom-call(bf16[32,32,1024]{2,1,0:T(8,128)(2,1)} %bitcast.9), custom_call_target="tpu_custom_call" | custom-call | tf_op jit(solution)/shard_map/return_rows/pallas_call | solution.py:137
  196.1 0.0 copy-done.5
  196.1 0.0 copy-start
  196.1 1.6 copy-done
  197.7 2.4 %place_rows.1 = bf16[32,32,1024]{2,1,0:T(8,128)(2,1)} custom-call(s32[32]{0:T(128)S(1)} %copy-done.5, f32[64]{0:T(128)S(1)} %compare_select_fusion.2.level_ref, bf16[32,32,1024]{2,1,0:T(8,128)(2,1)S(1)} %copy-done), custom_call_target="tpu_custom_call" | custom-call | tf_op jit(solution)/shard_map/place_rows/pallas_call | solution.py:293
  (2 shorter events, 0.0 us)
Async XLA Ops:
  1.3 3.7 %copy-start.1 = (bf16[32,32,1024]{2,1,0:T(8,128)(2,1)S(1)}, bf16[32,32,1024]{2,1,0:T(8,128)(2,1)}, u32[]{:S(2)}) copy-start(bf16[32,32,1024]{2,1,0:T(8,128)(2,1)} %g_hbm.1) | copy-start | bytes 6291460
  5.1 1.6 copy-start.2
  6.6 2.2 %copy-start.3 = (f32[32,32,1024]{2,1,0:T(8,128)S(1)}, f32[32,32,1024]{2,1,0:T(8,128)}, u32[]{:S(2)}) copy-start(f32[32,32,1024]{2,1,0:T(8,128)} %m_hbm.1) | copy-start | bytes 12582916
  63.3 1.3 copy-start.4
  143.8 52.3 %copy-start.5 = (s32[32]{0:T(128)S(1)}, s32[32]{0:T(128)}, u32[]{:S(2)}) copy-start(s32[32]{0:T(128)} %assign_ref.1) | copy-start | bytes 388
  196.1 1.6 copy-start

commit v2 on v1

v2 whole, which is shorter than its diff:
```python
import functools
import math

import jax
import jax.numpy as jnp
from jax import lax
from jax.experimental import pallas as pl
from jax.experimental.pallas import tpu as pltpu
from jax.sharding import PartitionSpec as P

MESH = pl.DeviceIdType.MESH
ANY = pl.BlockSpec(memory_space=pl.ANY)
VMEM = pl.BlockSpec(memory_space=pltpu.VMEM)
SMEM = pl.BlockSpec(memory_space=pltpu.SMEM)
F32 = jnp.float32
BF16 = jnp.bfloat16
VMEM_BYTES = 56 << 20


def dot(a, b):
    return jnp.dot(a, b, preferred_element_type=F32)


def peers(fsdp_count, owner_count):
    half = fsdp_count // 2
    stride = next(k for k in range(half + 1, 2 * fsdp_count) if math.gcd(k, fsdp_count) == 1)
    fsdp, owner = lax.axis_index("fsdp"), lax.axis_index("owner")

    def wrap(value, count):
        return jnp.where(value >= count, value - count, value)

    for step in range(fsdp_count * owner_count):
        inner = step % fsdp_count
        fsdp_off = (half + stride * inner) % fsdp_count
        owner_off = (step // fsdp_count + inner) % owner_count
        if fsdp_off or owner_off:
            yield wrap(fsdp + fsdp_off, fsdp_count), wrap(owner + owner_off, owner_count)


def position(owner_count):
    return lax.axis_index("fsdp") * owner_count + lax.axis_index("owner")


def send_all(fsdp_count, owner_count, x_ref, o_ref, send_sem, recv_sem):
    me = position(owner_count)
    for fsdp, owner in peers(fsdp_count, owner_count):
        pltpu.make_async_remote_copy(
            src_ref=x_ref.at[fsdp * owner_count + owner],
            dst_ref=o_ref.at[me],
            send_sem=send_sem,
            recv_sem=recv_sem,
            device_id=(fsdp, owner),
            device_id_type=MESH,
        ).start()


def wait_all(x_ref, o_ref, send_sem, recv_sem):
    most = pl.ds(0, o_ref.shape[0] - 1)
    pltpu.make_async_copy(o_ref.at[most], o_ref.at[most], recv_sem).wait()
    pltpu.make_async_copy(x_ref.at[most], x_ref.at[most], send_sem).wait()


def greet_all(fsdp_count, owner_count):
    barrier = pltpu.get_barrier_semaphore()
    for peer in peers(fsdp_count, owner_count):
        pl.semaphore_signal(barrier, inc=1, device_id=peer, device_id_type=MESH)


def greeted(fsdp_count, owner_count):
    pl.semaphore_wait(pltpu.get_barrier_semaphore(), fsdp_count * owner_count - 1)


def gather_kernel(
    fsdp_count, owner_count, g_hbm, m_hbm, assign_ref, o_ref, parts_ref,
    g_ref, m_ref, out_ref, sums, stage, row_sem, part_sem, own_sem, load_sem,
):
    me = position(owner_count)
    load_g = pltpu.make_async_copy(g_hbm, g_ref, load_sem.at[0])
    load_m = pltpu.make_async_copy(m_hbm, m_ref, load_sem.at[1])
    load_g.start()
    load_m.start()
    greet_all(fsdp_count, owner_count)
    count, row_count, width = g_ref.shape
    load_g.wait()

    def rows_by_slot(slot, carry):
        out_ref[slot] = g_ref[assign_ref[slot]]
        return carry

    lax.fori_loop(0, count, rows_by_slot, 0)
    own = pltpu.make_async_copy(out_ref.at[me], o_ref.at[me], own_sem.at[0])
    own.start()
    greeted(fsdp_count, owner_count)
    send_all(fsdp_count, owner_count, out_ref, o_ref, row_sem.at[0], row_sem.at[1])
    load_m.wait()

    def adam(block, carry):
        wide = g_ref[block].astype(F32)
        moment = 0.9 * m_ref[block] + 0.1 * wide * wide
        adam_dir = wide / (jnp.sqrt(moment) + 1e-08)
        folded = jnp.sum((adam_dir * adam_dir).reshape(row_count // 8, 8, width), axis=0)
        sums[block] = sum(folded[:, at : at + 128] for at in range(0, width, 128))
        return carry

    lax.fori_loop(0, count, adam, 0)

    def parts_by_slot(slot, carry):
        stage[slot] = sums[assign_ref[slot]]
        return carry

    lax.fori_loop(0, count, parts_by_slot, 0)
    own_part = pltpu.make_async_copy(stage.at[me], parts_ref.at[me], own_sem.at[1])
    own_part.start()
    send_all(fsdp_count, owner_count, stage, parts_ref, part_sem.at[0], part_sem.at[1])
    own.wait()
    own_part.wait()
    wait_all(out_ref, o_ref, row_sem.at[0], row_sem.at[1])
    wait_all(stage, parts_ref, part_sem.at[0], part_sem.at[1])


def return_kernel(fsdp_count, owner_count, x_ref, o_ref, row_sem, own_sem):
    me = position(owner_count)
    greet_all(fsdp_count, owner_count)
    own = pltpu.make_async_copy(x_ref.at[me], o_ref.at[me], own_sem)
    own.start()
    greeted(fsdp_count, owner_count)
    send_all(fsdp_count, owner_count, x_ref, o_ref, row_sem.at[0], row_sem.at[1])
    own.wait()
    wait_all(x_ref, o_ref, row_sem.at[0], row_sem.at[1])


def gather_rows(grads, second_moment, assign, fsdp_count, owner_count):
    count = fsdp_count * owner_count
    part = (count, 8, 128)
    return pl.pallas_call(
        functools.partial(gather_kernel, fsdp_count, owner_count),
        out_shape=(
            jax.ShapeDtypeStruct(grads.shape, BF16),
            jax.ShapeDtypeStruct(part, F32),
        ),
        in_specs=[ANY, ANY, SMEM],
        out_specs=(ANY, ANY),
        scratch_shapes=[
            pltpu.VMEM(grads.shape, BF16),
            pltpu.VMEM(second_moment.shape, F32),
            pltpu.VMEM(grads.shape, BF16),
            pltpu.VMEM(part, F32),
            pltpu.VMEM(part, F32),
            pltpu.SemaphoreType.DMA((2,)),
            pltpu.SemaphoreType.DMA((2,)),
            pltpu.SemaphoreType.DMA((2,)),
            pltpu.SemaphoreType.DMA((2,)),
        ],
        compiler_params=pltpu.CompilerParams(
            collective_id=0, has_side_effects=True, vmem_limit_bytes=VMEM_BYTES
        ),
        name="gather_rows",
    )(grads, second_moment, assign)


def return_rows(blocks, fsdp_count, owner_count):
    return pl.pallas_call(
        functools.partial(return_kernel, fsdp_count, owner_count),
        out_shape=jax.ShapeDtypeStruct(blocks.shape, BF16),
        in_specs=[ANY],
        out_specs=ANY,
        scratch_shapes=[
            pltpu.SemaphoreType.DMA((2,)),
            pltpu.SemaphoreType.DMA,
        ],
        compiler_params=pltpu.CompilerParams(
            collective_id=1, has_side_effects=True, vmem_limit_bytes=VMEM_BYTES
        ),
        name="return_rows",
    )(blocks)


def scatter_kernel(assign_ref, x_ref, o_ref, held, load_sem, store_sem):
    def load(slot):
        return pltpu.make_async_copy(x_ref.at[slot], held.at[slot], load_sem.at[slot])

    def store(slot):
        return pltpu.make_async_copy(
            held.at[slot], o_ref.at[assign_ref[slot]], store_sem.at[slot]
        )

    def fill(slot, carry):
        load(slot).start()
        return carry

    def turn(slot, carry):
        load(slot).wait()
        store(slot).start()
        return carry

    def drain(slot, carry):
        store(slot).wait()
        return carry

    for body in (fill, turn, drain):
        lax.fori_loop(0, x_ref.shape[0], body, 0)


def scatter_rows(assign, x):
    return pl.pallas_call(
        scatter_kernel,
        out_shape=jax.ShapeDtypeStruct(x.shape, x.dtype),
        in_specs=[SMEM, ANY],
        out_specs=ANY,
        scratch_shapes=[
            pltpu.VMEM(x.shape, x.dtype),
            pltpu.SemaphoreType.DMA((x.shape[0],)),
            pltpu.SemaphoreType.DMA((x.shape[0],)),
        ],
        compiler_params=pltpu.CompilerParams(vmem_limit_bytes=VMEM_BYTES),
        name="scatter_rows",
    )(assign, x)


def owner_kernel(
    g_ref, ls_hbm, rs_hbm, parts_ref, ln_hbm, rn_hbm, out_ref,
    ls, rs, gt, low, mix, square, fourth, root, precond, load_sem, store_sem,
):
    size = g_ref.shape[0]
    tile = size // 2
    tiles = size // tile
    stats = (ls, rs)
    loads = [
        pltpu.make_async_copy(ls_hbm, ls, load_sem.at[0]),
        pltpu.make_async_copy(rs_hbm, rs, load_sem.at[1]),
    ]
    for load in loads:
        load.start()

    def diagonal(step, height):
        rows = lax.broadcasted_iota(jnp.int32, (height, size), 0) + step * height
        cols = lax.broadcasted_iota(jnp.int32, (height, size), 1)
        return rows == cols

    def rows_of(step, height=tile):
        return pl.ds(pl.multiple_of(step * height, height), height)

    gt[...] = g_ref[...].T
    for load in loads:
        load.wait()

    def gram(step, carry):
        here = rows_of(step)
        eye = jnp.where(diagonal(step, tile), 0.0001, 0.0).astype(F32)
        left = 0.9 * ls[here, :] + 0.1 * dot(g_ref[here, :], gt[...]) + eye
        ls[here, :] = left
        right = 0.9 * rs[here, :] + 0.1 * dot(gt[here, :], g_ref[...]) + eye
        rs[here, :] = right
        return (
            carry[0] + jnp.sum(left * left, axis=0, keepdims=True),
            carry[1] + jnp.sum(right * right, axis=0, keepdims=True),
        )

    zero = jnp.zeros((1, size), F32)
    sums = lax.fori_loop(0, tiles, gram, (zero, zero))
    stores = [
        pltpu.make_async_copy(ls, ln_hbm, store_sem.at[0]),
        pltpu.make_async_copy(rs, rn_hbm, store_sem.at[1]),
    ]
    for store in stores:
        store.start()
    frobs = [jnp.sqrt(jnp.sum(total, axis=1, keepdims=True)) for total in sums]
    inverses = [1.0 / frob for frob in frobs]
    scales = [lax.rsqrt(jnp.sqrt(frob)) for frob in frobs]

    def first(step, carry):
        here = rows_of(step, 128)
        eye = jnp.where(diagonal(step, 128), 5.0, 0.0).astype(F32)
        for side in range(2):
            matrix = stats[side][here, :] * inverses[side]
            newton = (eye - matrix) * 0.25
            low[side, here, :] = matrix.astype(BF16)
            mix[side, here, :] = newton.astype(BF16)
            root[side, here, :] = (scales[side] * newton).astype(BF16)
        return carry

    lax.fori_loop(0, size // 128, first, 0)

    def product(a, b, out, finish):
        def body(step, carry):
            here = rows_of(step)
            for side in range(2):
                out[side, here, :] = finish(step, dot(a[side, here, :], b[side])).astype(BF16)
            return carry

        lax.fori_loop(0, tiles, body, 0)

    def as_is(step, value):
        return value

    def newton_mix(step, value):
        return (jnp.where(diagonal(step, tile), 5.0, 0.0).astype(F32) - value) * 0.25

    product(mix, mix, square, as_is)
    product(square, square, fourth, as_is)
    product(fourth, low, mix, newton_mix)
    product(root, mix, square, as_is)

    def apply_left(step, carry):
        here = rows_of(step)
        gt[here, :] = dot(square[0, here, :], g_ref[...]).astype(BF16)
        return carry

    lax.fori_loop(0, tiles, apply_left, 0)

    def apply_right(step, carry):
        here = rows_of(step)
        value = dot(gt[here, :], square[1])
        precond[here, :] = value.astype(BF16)
        return carry + jnp.sum(value * value, axis=0, keepdims=True)

    squares = lax.fori_loop(0, tiles, apply_right, zero)
    precond_sq = jnp.sum(squares, axis=1, keepdims=True) / (size * size)
    parts = jnp.sum(parts_ref[...], axis=0)
    parts = jnp.sum(parts, axis=0, keepdims=True)
    adam_sq = jnp.sum(parts, axis=1, keepdims=True) / (size * size)
    graft = jnp.sqrt(adam_sq) / jnp.sqrt(precond_sq + 1e-06)

    def rescale(step, carry):
        here = rows_of(step, 128)
        out_ref[here, :] = (precond[here, :].astype(F32) * graft).astype(BF16)
        return carry

    lax.fori_loop(0, size // 128, rescale, 0)
    for store in stores:
        store.wait()


def owner_update(block, left_stat, right_stat, parts):
    shape = block.shape
    pair = (2,) + shape
    return pl.pallas_call(
        owner_kernel,
        out_shape=(
            jax.ShapeDtypeStruct(shape, F32),
            jax.ShapeDtypeStruct(shape, F32),
            jax.ShapeDtypeStruct(shape, BF16),
        ),
        in_specs=[VMEM, ANY, ANY, VMEM],
        out_specs=(ANY, ANY, VMEM),
        scratch_shapes=[
            pltpu.VMEM(shape, F32),
            pltpu.VMEM(shape, F32),
            pltpu.VMEM(shape, BF16),
            pltpu.VMEM(pair, BF16),
            pltpu.VMEM(pair, BF16),
            pltpu.VMEM(pair, BF16),
            pltpu.VMEM(pair, BF16),
            pltpu.VMEM(pair, BF16),
            pltpu.VMEM(shape, BF16),
            pltpu.SemaphoreType.DMA((2,)),
            pltpu.SemaphoreType.DMA((2,)),
        ],
        compiler_params=pltpu.CompilerParams(vmem_limit_bytes=VMEM_BYTES),
        name="owner_update",
    )(block, left_stat, right_stat, parts)


def local(fsdp_count, owner_count, grads, second_moment, assign, left_stats, right_stats):
    size = grads.shape[2]
    received, parts = gather_rows(grads, second_moment, assign, fsdp_count, owner_count)
    left_new, right_new, update = owner_update(
        received.reshape(size, size), left_stats[0], right_stats[0], parts
    )
    arrived = return_rows(update.reshape(grads.shape), fsdp_count, owner_count)
    return (scatter_rows(assign, arrived), left_new[None], right_new[None])


def solution(mesh):
    rows = P(None, ("fsdp", "owner"), None)
    blocks = P(("fsdp", "owner"), None, None)
    return jax.shard_map(
        functools.partial(local, mesh.shape["fsdp"], mesh.shape["owner"]),
        mesh=mesh,
        in_specs=(rows, rows, P(), blocks, blocks),
        out_specs=(rows, blocks, blocks),
        check_vma=False,
    )
```

time: 200 us -> 151 us (0.76)
  blocking collectives: 39 us -> 0 us
  local copies, waits for them, and re-layouts: 10.4 us -> 0 us
  Pallas kernels: 147 us -> 150 us
  other arithmetic: 2.82 us -> 0 us
    psum x1 -> x0, blocking collectives: 39 us -> none  [local(): lax.psum(jnp.concatenate([jnp.sum(sums, axis=1), mine]), ('fsdp', 'owner'))]
    unnamed x12 -> x0, local copies, waits for them, and re-layouts: 6.69 us -> none
    gather x1 -> x0, local copies, waits for them, and re-layouts: 3.74 us -> none  [local(): grads[assign]]
    pallas_call x1, Pallas kernels: 54.5 us -> 57.2 us  [gather_rows(): pl.pallas_call(functools.partial(gather_kernel, fsdp_count, owner_count),...]
where the time goes in v2:
time: 151 us; the launch traced here: 150 us
  Pallas kernels  150 us (99%)
    pallas_call x1, Pallas kernels, gather_rows(): pl.pallas_call(functools.partial(gather_kernel, fsdp_count, owner_count),...  57.2 us
    pallas_call x1, Pallas kernels, return_rows(): pl.pallas_call(functools.partial(return_kernel, fsdp_count, owner_count),...  50.5 us
    pallas_call x1, Pallas kernels, owner_update(): pl.pallas_call(owner_kernel, out_shape=(jax.ShapeDtypeStruct(shape, F32),...  38.4 us
    pallas_call x1, Pallas kernels, scatter_rows(): pl.pallas_call(scatter_kernel, out_shape=jax.ShapeDtypeStruct(x.shape, x....  3.46 us

profile of v2, /device:TPU:0, one launch (start us, length us, event | category | flops | bytes accessed | tf_op | source)
XLA Modules:
  0.0 150.3 jit_solution(4438539118795986561)
XLA Ops:
  0.6 57.2 %gather_rows.1 = (bf16[32,32,1024]{2,1,0:T(8,128)(2,1)}, f32[32,8,128]{2,1,0:T(8,128)}) custom-call(bf16[32,32,1024]{2,1,0:T(8,128)(2,1)} %g_hbm.1, f32[32,32,1024]{2,1,0:T(8,128)} %m_hbm.1, s32[32]{0:T(128)} %assign_ref.3), custom_call_target="tpu_custom_call" | custom-call | tf_op jit(solution)/shard_map/gather_rows/pallas_call | solution.py:135
  57.9 38.4 %owner_update.1 = (f32[1024,1024]{1,0:T(8,128)}, f32[1024,1024]{1,0:T(8,128)}, bf16[1024,1024]{1,0:T(8,128)(2,1)}) custom-call(bf16[1024,1024]{1,0:T(8,128)(2,1)} %bitcast.9, f32[1024,1024]{1,0:T(8,128)} %bitcast.6, f32[1024,1024]{1,0:T(8,128)} %bitcast.7, f32[32,8,128]{2,1,0:T(8,128)} %get-tuple-element.9.parts_ref), custom_call_target="tpu_custom_call" | custom-call | tf_op jit(solution)/shard_map/owner_update/pallas_call | solution.py:337
  96.3 50.5 %return_rows.1.x_ref = bf16[32,32,1024]{2,1,0:T(8,128)(2,1)} custom-call(bf16[32,32,1024]{2,1,0:T(8,128)(2,1)} %bitcast.8), custom_call_target="tpu_custom_call" | custom-call | tf_op jit(solution)/shard_map/return_rows/pallas_call | solution.py:162
  146.8 3.5 %scatter_rows.1 = bf16[32,32,1024]{2,1,0:T(8,128)(2,1)} custom-call(s32[32]{0:T(128)} %assign_ref.3, bf16[32,32,1024]{2,1,0:T(8,128)(2,1)} %return_rows.1.x_ref), custom_call_target="tpu_custom_call" | custom-call | tf_op jit(solution)/shard_map/scatter_rows/pallas_call | solution.py:205

commit v3 on v2

--- a/solution.py
+++ b/solution.py
@@ -15,6 +15,9 @@
 F32 = jnp.float32
 BF16 = jnp.bfloat16
 VMEM_BYTES = 56 << 20
+TILES = 1
+PIECE = 256
+CHUNK = 32
 
 
 def dot(a, b):
@@ -222,111 +225,131 @@
     ls, rs, gt, low, mix, square, fourth, root, precond, load_sem, store_sem,
 ):
     size = g_ref.shape[0]
-    tile = size // 2
-    tiles = size // tile
+    tile = size // TILES
     stats = (ls, rs)
     loads = [
         pltpu.make_async_copy(ls_hbm, ls, load_sem.at[0]),
         pltpu.make_async_copy(rs_hbm, rs, load_sem.at[1]),
     ]
-    for load in loads:
-        load.start()
-
-    def diagonal(step, height):
-        rows = lax.broadcasted_iota(jnp.int32, (height, size), 0) + step * height
-        cols = lax.broadcasted_iota(jnp.int32, (height, size), 1)
-        return rows == cols
-
-    def rows_of(step, height=tile):
-        return pl.ds(pl.multiple_of(step * height, height), height)
-
-    gt[...] = g_ref[...].T
-    for load in loads:
-        load.wait()
-
-    def gram(step, carry):
-        here = rows_of(step)
-        eye = jnp.where(diagonal(step, tile), 0.0001, 0.0).astype(F32)
-        left = 0.9 * ls[here, :] + 0.1 * dot(g_ref[here, :], gt[...]) + eye
-        ls[here, :] = left
-        right = 0.9 * rs[here, :] + 0.1 * dot(gt[here, :], g_ref[...]) + eye
-        rs[here, :] = right
-        return (
-            carry[0] + jnp.sum(left * left, axis=0, keepdims=True),
-            carry[1] + jnp.sum(right * right, axis=0, keepdims=True),
-        )
-
-    zero = jnp.zeros((1, size), F32)
-    sums = lax.fori_loop(0, tiles, gram, (zero, zero))
     stores = [
         pltpu.make_async_copy(ls, ln_hbm, store_sem.at[0]),
         pltpu.make_async_copy(rs, rn_hbm, store_sem.at[1]),
     ]
-    for store in stores:
-        store.start()
-    frobs = [jnp.sqrt(jnp.sum(total, axis=1, keepdims=True)) for total in sums]
-    inverses = [1.0 / frob for frob in frobs]
-    scales = [lax.rsqrt(jnp.sqrt(frob)) for frob in frobs]
-
-    def first(step, carry):
-        here = rows_of(step, 128)
-        eye = jnp.where(diagonal(step, 128), 5.0, 0.0).astype(F32)
-        for side in range(2):
-            matrix = stats[side][here, :] * inverses[side]
-            newton = (eye - matrix) * 0.25
-            low[side, here, :] = matrix.astype(BF16)
-            mix[side, here, :] = newton.astype(BF16)
-            root[side, here, :] = (scales[side] * newton).astype(BF16)
-        return carry
-
-    lax.fori_loop(0, size // 128, first, 0)
-
-    def product(a, b, out, finish):
+    for load in loads:
+        load.start()
+
+    def rows_of(step, height):
+        return pl.ds(pl.multiple_of(step * height, height), height)
+
+    def diagonal(start, height, at, width, value):
+        rows = lax.broadcasted_iota(jnp.int32, (height, width), 0) + start
+        cols = lax.broadcasted_iota(jnp.int32, (height, width), 1) + at
+        return jnp.where(rows == cols, value, 0.0).astype(F32)
+
+    def product(a, b, finish):
+        def run(step, carry):
+            rows = a[rows_of(step, tile), :]
+            for at in range(0, size, PIECE):
+                carry = finish(step, at, dot(rows, b[:, at : at + PIECE]), carry)
+            return carry
+
+        return run
+
+    def keep(out):
+        def finish(step, at, value, carry):
+            out[rows_of(step, tile), at : at + PIECE] = value.astype(BF16)
+            return carry
+
+        return finish
+
+    def newton_mix(out):
+        def finish(step, at, value, carry):
+            mixed = (diagonal(step * tile, tile, at, PIECE, 5.0) - value) * 0.25
+            out[rows_of(step, tile), at : at + PIECE] = mixed.astype(BF16)
+            return carry
+
+        return finish
+
+    def statistics(stat):
+        def finish(step, at, value, carry):
+            here, cols = rows_of(step, tile), slice(at, at + PIECE)
+            eye = diagonal(step * tile, tile, at, PIECE, 0.0001)
+            new = 0.9 * stat[here, cols] + 0.1 * value + eye
+            stat[here, cols] = new
+            return carry + jnp.sum((new * new).reshape(tile // 8, 8, PIECE), axis=0)
+
+        return finish
+
+    def stage(*works):
         def body(step, carry):
-            here = rows_of(step)
-            for side in range(2):
-                out[side, here, :] = finish(step, dot(a[side, here, :], b[side])).astype(BF16)
+            return tuple(work(step, part) for work, part in zip(works, carry))
+
+        zero = jnp.zeros((8, PIECE), F32)
+        return lax.fori_loop(0, TILES, body, (zero,) * len(works))
+
+    def total(partial):
+        return jnp.sum(jnp.sum(partial, axis=0, keepdims=True), axis=1, keepdims=True)
+
+    def first(side, squares):
+        frob = jnp.sqrt(total(squares))
+        inverse = 1.0 / frob
+        scale = lax.rsqrt(jnp.sqrt(frob))
+
+        def run(step, carry):
+            for part in range(tile // CHUNK):
+                start = step * tile + part * CHUNK
+                here = pl.ds(pl.multiple_of(start, CHUNK), CHUNK)
+                matrix = stats[side][here, :] * inverse
+                newton = (diagonal(start, CHUNK, 0, size, 5.0) - matrix) * 0.25
+                low[side, here, :] = matrix.astype(BF16)
+                mix[side, here, :] = newton.astype(BF16)
+                root[side, here, :] = (scale * newton).astype(BF16)
             return carry
 
-        lax.fori_loop(0, tiles, body, 0)
-
-    def as_is(step, value):
-        return value
-
-    def newton_mix(step, value):
-        return (jnp.where(diagonal(step, tile), 5.0, 0.0).astype(F32) - value) * 0.25
-
-    product(mix, mix, square, as_is)
-    product(square, square, fourth, as_is)
-    product(fourth, low, mix, newton_mix)
-    product(root, mix, square, as_is)
-
-    def apply_left(step, carry):
-        here = rows_of(step)
-        gt[here, :] = dot(square[0, here, :], g_ref[...]).astype(BF16)
-        return carry
-
-    lax.fori_loop(0, tiles, apply_left, 0)
-
-    def apply_right(step, carry):
-        here = rows_of(step)
-        value = dot(gt[here, :], square[1])
-        precond[here, :] = value.astype(BF16)
-        return carry + jnp.sum(value * value, axis=0, keepdims=True)
-
-    squares = lax.fori_loop(0, tiles, apply_right, zero)
-    precond_sq = jnp.sum(squares, axis=1, keepdims=True) / (size * size)
-    parts = jnp.sum(parts_ref[...], axis=0)
-    parts = jnp.sum(parts, axis=0, keepdims=True)
-    adam_sq = jnp.sum(parts, axis=1, keepdims=True) / (size * size)
+        return run
+
+    gt[...] = g_ref[...].T
+    loads[0].wait()
+    (left_sq,) = stage(product(g_ref, gt, statistics(ls)))
+    stores[0].start()
+    loads[1].wait()
+    right_sq, _ = stage(product(gt, g_ref, statistics(rs)), first(0, left_sq))
+    stores[1].start()
+    mixes, lows, roots = ([ref.at[side] for side in range(2)] for ref in (mix, low, root))
+    squares, fourths = ([ref.at[side] for side in range(2)] for ref in (square, fourth))
+    stage(product(mixes[0], mixes[0], keep(squares[0])), first(1, right_sq))
+    stage(
+        product(mixes[1], mixes[1], keep(squares[1])),
+        product(squares[0], squares[0], keep(fourths[0])),
+    )
+    stage(
+        product(squares[1], squares[1], keep(fourths[1])),
+        product(fourths[0], lows[0], newton_mix(mixes[0])),
+    )
+    stage(
+        product(fourths[1], lows[1], newton_mix(mixes[1])),
+        product(roots[0], mixes[0], keep(squares[0])),
+    )
+    stage(
+        product(roots[1], mixes[1], keep(squares[1])),
+        product(squares[0], g_ref, keep(gt)),
+    )
+
+    def last(step, at, value, carry):
+        precond[rows_of(step, tile), at : at + PIECE] = value.astype(BF16)
+        return carry + jnp.sum((value * value).reshape(tile // 8, 8, PIECE), axis=0)
+
+    (precond_squares,) = stage(product(gt, squares[1], last))
+    precond_sq = total(precond_squares) / (size * size)
+    adam_sq = total(jnp.sum(parts_ref[...], axis=0)) / (size * size)
     graft = jnp.sqrt(adam_sq) / jnp.sqrt(precond_sq + 1e-06)
 
     def rescale(step, carry):
-        here = rows_of(step, 128)
+        here = rows_of(step, CHUNK)
         out_ref[here, :] = (precond[here, :].astype(F32) * graft).astype(BF16)
         return carry
 
-    lax.fori_loop(0, size // 128, rescale, 0)
+    lax.fori_loop(0, size // CHUNK, rescale, 0)
     for store in stores:
         store.wait()
 

time: 151 us -> 145 us (0.960)
  Pallas kernels: 150 us -> 144 us
    pallas_call x1, Pallas kernels: 38.4 us -> 32.8 us  [owner_update(): pl.pallas_call(owner_kernel, out_shape=(jax.ShapeDtypeStruct(shape, F32),...]
where the time goes in v3:
time: 145 us
  Pallas kernels  144 us (99%)
    pallas_call x1, Pallas kernels, gather_rows(): pl.pallas_call(functools.partial(gather_kernel, fsdp_count, owner_count),...  57.2 us
    pallas_call x1, Pallas kernels, return_rows(): pl.pallas_call(functools.partial(return_kernel, fsdp_count, owner_count),...  50.5 us
    pallas_call x1, Pallas kernels, owner_update(): pl.pallas_call(owner_kernel, out_shape=(jax.ShapeDtypeStruct(shape, F32),...  32.8 us
    pallas_call x1, Pallas kernels, scatter_rows(): pl.pallas_call(scatter_kernel, out_shape=jax.ShapeDtypeStruct(x.shape, x....  3.46 us

profile of v3, /device:TPU:0, one launch (start us, length us, event | category | flops | bytes accessed | tf_op | source)
XLA Modules:
  0.0 144.8 jit_solution(4235532095141768926)
XLA Ops:
  0.6 57.2 %gather_rows.1 = (bf16[32,32,1024]{2,1,0:T(8,128)(2,1)}, f32[32,8,128]{2,1,0:T(8,128)}) custom-call(bf16[32,32,1024]{2,1,0:T(8,128)(2,1)} %g_hbm.1, f32[32,32,1024]{2,1,0:T(8,128)} %m_hbm.1, s32[32]{0:T(128)} %assign_ref.3), custom_call_target="tpu_custom_call" | custom-call | tf_op jit(solution)/shard_map/gather_rows/pallas_call | solution.py:138
  57.9 32.8 %owner_update.1 = (f32[1024,1024]{1,0:T(8,128)}, f32[1024,1024]{1,0:T(8,128)}, bf16[1024,1024]{1,0:T(8,128)(2,1)}) custom-call(bf16[1024,1024]{1,0:T(8,128)(2,1)} %bitcast.9, f32[1024,1024]{1,0:T(8,128)} %bitcast.6, f32[1024,1024]{1,0:T(8,128)} %bitcast.7, f32[32,8,128]{2,1,0:T(8,128)} %get-tuple-element.9.parts_ref), custom_call_target="tpu_custom_call" | custom-call | tf_op jit(solution)/shard_map/owner_update/pallas_call | solution.py:360
  90.7 50.5 %return_rows.1.x_ref = bf16[32,32,1024]{2,1,0:T(8,128)(2,1)} custom-call(bf16[32,32,1024]{2,1,0:T(8,128)(2,1)} %bitcast.8), custom_call_target="tpu_custom_call" | custom-call | tf_op jit(solution)/shard_map/return_rows/pallas_call | solution.py:165
  141.2 3.5 %scatter_rows.1 = bf16[32,32,1024]{2,1,0:T(8,128)(2,1)} custom-call(s32[32]{0:T(128)} %assign_ref.3, bf16[32,32,1024]{2,1,0:T(8,128)(2,1)} %return_rows.1.x_ref), custom_call_target="tpu_custom_call" | custom-call | tf_op jit(solution)/shard_map/scatter_rows/pallas_call | solution.py:208

commit v4 on v3

--- a/solution.py
+++ b/solution.py
@@ -81,10 +81,10 @@
     load_g = pltpu.make_async_copy(g_hbm, g_ref, load_sem.at[0])
     load_m = pltpu.make_async_copy(m_hbm, m_ref, load_sem.at[1])
     load_g.start()
-    load_m.start()
     greet_all(fsdp_count, owner_count)
     count, row_count, width = g_ref.shape
     load_g.wait()
+    load_m.start()
 
     def rows_by_slot(slot, carry):
         out_ref[slot] = g_ref[assign_ref[slot]]
@@ -345,11 +345,11 @@
     graft = jnp.sqrt(adam_sq) / jnp.sqrt(precond_sq + 1e-06)
 
     def rescale(step, carry):
-        here = rows_of(step, CHUNK)
+        here = rows_of(step, 4 * CHUNK)
         out_ref[here, :] = (precond[here, :].astype(F32) * graft).astype(BF16)
         return carry
 
-    lax.fori_loop(0, size // CHUNK, rescale, 0)
+    lax.fori_loop(0, size // (4 * CHUNK), rescale, 0)
     for store in stores:
         store.wait()
 

time: 145 us -> 145 us (level)
  no operation moved by 1% of the time
where the time goes in v4:
time: 145 us
  Pallas kernels  144 us (99%)
    pallas_call x1, Pallas kernels, gather_rows(): pl.pallas_call(functools.partial(gather_kernel, fsdp_count, owner_count),...  57.2 us
    pallas_call x1, Pallas kernels, return_rows(): pl.pallas_call(functools.partial(return_kernel, fsdp_count, owner_count),...  50.5 us
    pallas_call x1, Pallas kernels, owner_update(): pl.pallas_call(owner_kernel, out_shape=(jax.ShapeDtypeStruct(shape, F32),...  32.7 us
    pallas_call x1, Pallas kernels, scatter_rows(): pl.pallas_call(scatter_kernel, out_shape=jax.ShapeDtypeStruct(x.shape, x....  3.46 us

profile of v4, /device:TPU:0, one launch (start us, length us, event | category | flops | bytes accessed | tf_op | source)
XLA Modules:
  0.0 144.7 jit_solution(4588359907562919460)
XLA Ops:
  0.6 57.2 %gather_rows.1 = (bf16[32,32,1024]{2,1,0:T(8,128)(2,1)}, f32[32,8,128]{2,1,0:T(8,128)}) custom-call(bf16[32,32,1024]{2,1,0:T(8,128)(2,1)} %g_hbm.1, f32[32,32,1024]{2,1,0:T(8,128)} %m_hbm.1, s32[32]{0:T(128)} %assign_ref.3), custom_call_target="tpu_custom_call" | custom-call | tf_op jit(solution)/shard_map/gather_rows/pallas_call | solution.py:138
  57.9 32.7 %owner_update.1 = (f32[1024,1024]{1,0:T(8,128)}, f32[1024,1024]{1,0:T(8,128)}, bf16[1024,1024]{1,0:T(8,128)(2,1)}) custom-call(bf16[1024,1024]{1,0:T(8,128)(2,1)} %bitcast.9, f32[1024,1024]{1,0:T(8,128)} %bitcast.6, f32[1024,1024]{1,0:T(8,128)} %bitcast.7, f32[32,8,128]{2,1,0:T(8,128)} %get-tuple-element.9.parts_ref), custom_call_target="tpu_custom_call" | custom-call | tf_op jit(solution)/shard_map/owner_update/pallas_call | solution.py:360
  90.5 50.5 %return_rows.1.x_ref = bf16[32,32,1024]{2,1,0:T(8,128)(2,1)} custom-call(bf16[32,32,1024]{2,1,0:T(8,128)(2,1)} %bitcast.8), custom_call_target="tpu_custom_call" | custom-call | tf_op jit(solution)/shard_map/return_rows/pallas_call | solution.py:165
  141.0 3.5 %scatter_rows.1 = bf16[32,32,1024]{2,1,0:T(8,128)(2,1)} custom-call(s32[32]{0:T(128)} %assign_ref.3, bf16[32,32,1024]{2,1,0:T(8,128)(2,1)} %return_rows.1.x_ref), custom_call_target="tpu_custom_call" | custom-call | tf_op jit(solution)/shard_map/scatter_rows/pallas_call | solution.py:208
